TPU v7x, 32 devices: a whole 2x2x4 slice. The times are simulated.
32 devices in a mesh: dp: 16 (over z, x, core), tensor: 2 (over y).
Axes of the slice: x: 2, y: 2, z: 4, core: 2. Of those that a mesh axis runs over, the one named last changes fastest.
Arguments:
- tokens: bfloat16 [8192, 1024], P('dp'), may hold values from -6 to 6
- cotangent: bfloat16 [8192, 1024], P('dp'), may hold values from -6 to 6
- segment: int32 [8192], P('dp'), may hold values from 0 to 7, never falling along the last dimension, each value on 1 to 6144 neighbouring positions
- variate: int32 [8192], P('dp'), may hold values from 0 to 3
- time: int32 [8192], P('dp'), may hold values from 0 to 4095
- w_qkv: bfloat16 [3, 1024, 1024], P(None, None, 'tensor'), may hold values from -0.1875 to 0.1875
- w_out: bfloat16 [1024, 1024], P('tensor'), may hold values from -2 to 2
- w_gateup: bfloat16 [2, 1024, 2816], P(None, None, 'tensor'), may hold values from -0.1875 to 0.1875
- w_down: bfloat16 [2816, 1024], P('tensor'), may hold values from -0.109375 to 0.109375
- attn_gain: float32 [1024], replicated, may hold values from 0.5 to 1.5
- mlp_gain: float32 [1024], replicated, may hold values from 0.5 to 1.5
- query_gain: float32 [64], replicated, may hold values from 0.5 to 1.5
- key_gain: float32 [64], replicated, may hold values from 0.5 to 1.5
- var_bias: float32 [2, 16], P(None, 'tensor'), may hold values from -4 to 4
Outputs:
- output: bfloat16 [8192, 1024], P('dp', 'tensor')
- grad_input: float32 [8192, 1024], P('dp', 'tensor')
- grad_qkv: float32 [3, 1024, 1024], P(None, None, 'tensor')
- grad_out: float32 [1024, 1024], P('tensor')
- grad_gateup: float32 [2, 1024, 2816], P(None, None, 'tensor')
- grad_down: float32 [2816, 1024], P('tensor')
- grad_attn_gain: float32 [1024], replicated
- grad_mlp_gain: float32 [1024], replicated
- grad_query_gain: float32 [64], replicated
- grad_key_gain: float32 [64], replicated
- grad_var_bias: float32 [2, 16], P(None, 'tensor')
Inputs may be any that keep to these rules, and one draw needn't show every extreme that they name: `segment`: document numbers never fall along the tokens; all documents lie in the one packed sequence of 8192 tokens, each with at most 6144 tokens.
All inputs are finite; a program needn't handle non-finite values.
Results may differ from a plain program's by a relative error of at most 0.022.
Values may be sent and summed in bfloat16 or wider, within the bound.
A program may use at most 256 MiB of HBM per device.

v0:
```python
import jax
import jax.numpy as jnp
from jax import lax
from jax.sharding import PartitionSpec as P

HD = 64


EPSILON = 1e-05
MASKED = -1e30


def heads_view(rows):
    return rows.reshape(rows.shape[0], -1, HD)


def rotary_table(times):
    half_dim = HD // 2
    inverse = 10000.0 ** (-2.0 * jnp.arange(half_dim, dtype=jnp.float32) / HD)
    angles = times.astype(jnp.float32)[:, None] * inverse[None, :]
    return (jnp.cos(angles)[:, None, :], jnp.sin(angles)[:, None, :])


def rotate(values, cosine, sine_table):
    half_dim = values.shape[-1] // 2
    first_half = values[..., :half_dim]
    second_half = values[..., half_dim:]
    return jnp.concatenate(
        [
            first_half * cosine - second_half * sine_table,
            second_half * cosine + first_half * sine_table,
        ],
        axis=-1,
    )


def rotate_back(grads_in, cosine, sine_table):
    half_dim = grads_in.shape[-1] // 2
    first_half = grads_in[..., :half_dim]
    second_half = grads_in[..., half_dim:]
    return jnp.concatenate(
        [
            first_half * cosine + second_half * sine_table,
            second_half * cosine - first_half * sine_table,
        ],
        axis=-1,
    )


def block_scores(query_rows, query_segs, query_vars, key_rows, key_segs, key_vars, bias_table):
    raw_scores = jnp.einsum(
        "thd,uhd->htu",
        heads_view(query_rows),
        heads_view(key_rows),
        preferred_element_type=jnp.float32,
    ) * HD ** (-0.5)
    same_var = (query_vars[:, None] == key_vars[None, :])[None]
    allowed = (query_segs[:, None] == key_segs[None, :])[None]
    biased = raw_scores + jnp.where(
        same_var, bias_table[0][:, None, None], bias_table[1][:, None, None]
    )
    return (jnp.where(allowed, biased, MASKED), allowed, same_var)


def block_grads(
    query_rows,
    query_segs,
    query_vars,
    grad_rows,
    total_rows,
    delta_rows,
    key_rows,
    value_rows,
    key_segs,
    key_vars,
    bias_table,
):
    scores, allowed, same_var = block_scores(
        query_rows, query_segs, query_vars, key_rows, key_segs, key_vars, bias_table
    )
    probs = jnp.where(allowed, jnp.exp(scores - total_rows[:, :, None]), 0.0)
    grad_probs = jnp.einsum(
        "thd,uhd->htu",
        heads_view(grad_rows),
        heads_view(value_rows),
        preferred_element_type=jnp.float32,
    )
    grad_scores = (probs * (grad_probs - delta_rows[:, :, None])).astype(jnp.bfloat16)
    wide_scores = grad_scores.astype(jnp.float32)
    same_sum = jnp.sum(jnp.where(same_var, wide_scores, 0.0), axis=(1, 2))
    bias_part = jnp.stack([same_sum, jnp.sum(wide_scores, axis=(1, 2)) - same_sum])
    return (probs.astype(jnp.bfloat16), grad_scores, bias_part)


def shards(
    tokens,
    cotangent,
    segment,
    variate,
    time,
    w_qkv,
    w_out,
    w_gateup,
    w_down,
    attn_gain,
    mlp_gain,
    query_gain,
    key_gain,
    var_bias,
):
    tok_rows = tokens.shape[0]
    local_width = w_qkv.shape[2]
    heads_here = local_width // HD
    seq_rows = tok_rows * lax.axis_size("dp")
    block_keys = min(1024, seq_rows)
    block_count = seq_rows // block_keys
    seq_start = 0
    width_share = tokens.shape[1] // lax.axis_size("tensor")
    tensor_start = lax.axis_index("tensor") * width_share
    block_ids = jnp.arange(block_count, dtype=jnp.int32)
    inputs = tokens.astype(jnp.float32)
    scale_one = lax.rsqrt(jnp.mean(inputs * inputs, axis=1, keepdims=True) + EPSILON)
    unit_one = inputs * scale_one
    normed_one = (unit_one * attn_gain).astype(jnp.bfloat16)
    projected = jnp.einsum("td,kde->kte", normed_one, w_qkv, preferred_element_type=jnp.float32)
    cosine, sine_table = rotary_table(time)
    raw_query = heads_view(projected[0])
    raw_key = heads_view(projected[1])
    query_scale = lax.rsqrt(jnp.mean(raw_query * raw_query, axis=-1, keepdims=True) + EPSILON)
    key_scale = lax.rsqrt(jnp.mean(raw_key * raw_key, axis=-1, keepdims=True) + EPSILON)
    unit_query = raw_query * query_scale
    unit_key = raw_key * key_scale
    queries = (
        rotate(unit_query * query_gain, cosine, sine_table)
        .astype(jnp.bfloat16)
        .reshape(tok_rows, local_width)
    )
    keys_local = (
        rotate(unit_key * key_gain, cosine, sine_table)
        .astype(jnp.bfloat16)
        .reshape(tok_rows, local_width)
    )
    values_local = projected[2].astype(jnp.bfloat16)
    all_keys, all_values, all_segs, all_vars = (
        lax.all_gather(keys_local, "dp", axis=0, tiled=True),
        lax.all_gather(values_local, "dp", axis=0, tiled=True),
        lax.all_gather(segment, "dp", axis=0, tiled=True),
        lax.all_gather(variate, "dp", axis=0, tiled=True),
    )

    def key_block(index_block):
        begin_row = seq_start + index_block * block_keys
        return tuple(
            (
                lax.dynamic_slice_in_dim(whole_rows, begin_row, block_keys, 0)
                for whole_rows in (all_keys, all_values, all_segs, all_vars)
            )
        )

    def first_pass(carried, index_block):
        key_rows, value_rows, key_segs, key_vars = key_block(index_block)
        running_max, running_sum = carried
        scores, allowed, same_var = block_scores(
            queries, segment, variate, key_rows, key_segs, key_vars, var_bias
        )
        new_max = jnp.maximum(running_max, jnp.max(scores, axis=2))
        kept_terms = jnp.where(allowed, jnp.exp(scores - new_max[:, :, None]), 0.0)
        return (
            (new_max, running_sum * jnp.exp(running_max - new_max) + jnp.sum(kept_terms, axis=2)),
            None,
        )

    start_state = (
        jnp.full((heads_here, tok_rows), MASKED, jnp.float32),
        jnp.zeros((heads_here, tok_rows), jnp.float32),
    )
    (running_max, running_sum), unused = lax.scan(first_pass, start_state, block_ids)
    log_total = running_max + jnp.log(running_sum)

    def second_pass(carried, index_block):
        key_rows, value_rows, key_segs, key_vars = key_block(index_block)
        out_high, out_low = carried
        scores, allowed, same_var = block_scores(
            queries, segment, variate, key_rows, key_segs, key_vars, var_bias
        )
        probs = jnp.where(allowed, jnp.exp(scores - log_total[:, :, None]), 0.0)
        probs_low = probs.astype(jnp.bfloat16)
        rest_low = (probs - probs_low.astype(jnp.float32)).astype(jnp.bfloat16)
        value_heads = heads_view(value_rows)
        return (
            (
                out_high
                + jnp.einsum(
                    "htu,uhd->thd", probs_low, value_heads, preferred_element_type=jnp.float32
                ),
                out_low
                + jnp.einsum(
                    "htu,uhd->thd", rest_low, value_heads, preferred_element_type=jnp.float32
                ),
            ),
            None,
        )

    zero_heads = jnp.zeros((tok_rows, heads_here, HD), jnp.float32)
    (out_high, out_low), unused = lax.scan(second_pass, (zero_heads, zero_heads), block_ids)
    heads_out = out_high.reshape(tok_rows, local_width).astype(jnp.bfloat16)
    exact_out = (out_high + out_low).reshape(tok_rows, local_width)
    attn_part = jnp.dot(heads_out, w_out, preferred_element_type=jnp.float32)
    attn_total = lax.psum(attn_part, "tensor")
    middle = inputs + attn_total
    scale_two = lax.rsqrt(jnp.mean(middle * middle, axis=1, keepdims=True) + EPSILON)
    unit_two = middle * scale_two
    normed_two = (unit_two * mlp_gain).astype(jnp.bfloat16)
    gate_up = jnp.einsum("td,kdf->ktf", normed_two, w_gateup, preferred_element_type=jnp.float32)
    gate_vals = gate_up[0]
    up_vals = gate_up[1]
    sig_gate = jax.nn.sigmoid(gate_vals)
    act_gate = gate_vals * sig_gate
    hidden = (act_gate * up_vals).astype(jnp.bfloat16)
    mlp_part = jnp.dot(hidden, w_down, preferred_element_type=jnp.float32)
    mlp_share = lax.psum_scatter(mlp_part, "tensor", scatter_dimension=1, tiled=True)
    output = (lax.dynamic_slice_in_dim(middle, tensor_start, width_share, 1) + mlp_share).astype(
        jnp.bfloat16
    )
    grad_hidden = jnp.einsum("te,fe->tf", cotangent, w_down, preferred_element_type=jnp.float32)
    grad_down = jnp.einsum("tf,te->fe", hidden, cotangent, preferred_element_type=jnp.float32)
    grad_gate = grad_hidden * up_vals * sig_gate * (1.0 + gate_vals * (1.0 - sig_gate))
    grad_up = grad_hidden * act_gate
    grad_gu = jnp.stack([grad_gate, grad_up]).astype(jnp.bfloat16)
    grad_gateup = jnp.einsum("td,ktf->kdf", normed_two, grad_gu, preferred_element_type=jnp.float32)
    grad_normed_two = jnp.einsum(
        "ktf,kdf->td", grad_gu, w_gateup, preferred_element_type=jnp.float32
    )
    mlp_gain_part = jnp.sum(grad_normed_two * unit_two, axis=0)
    scaled_two = grad_normed_two * mlp_gain
    middle_part = scale_two * (
        scaled_two - unit_two * jnp.mean(scaled_two * unit_two, axis=1, keepdims=True)
    )
    middle_share = lax.psum_scatter(middle_part, "tensor", scatter_dimension=1, tiled=True)
    middle_share = (
        lax.dynamic_slice_in_dim(cotangent.astype(jnp.float32), tensor_start, width_share, 1)
        + middle_share
    )
    grad_middle = lax.all_gather(middle_share, "tensor", axis=1, tiled=True)
    grad_middle_low = grad_middle.astype(jnp.bfloat16)
    grad_out = jnp.einsum(
        "tc,td->cd", heads_out, grad_middle_low, preferred_element_type=jnp.float32
    )
    grad_heads = jnp.einsum(
        "td,cd->tc", grad_middle_low, w_out, preferred_element_type=jnp.float32
    ).astype(jnp.bfloat16)
    row_delta = jnp.sum(heads_view(grad_heads.astype(jnp.float32) * exact_out), axis=2).T
    zero_bias = jnp.zeros((2, heads_here), jnp.float32)

    def back_pass(carried, index_block):
        key_rows, value_rows, key_segs, key_vars = key_block(index_block)
        query_acc, bias_acc, key_acc, value_acc = carried
        probs_low, grad_scores, bias_part = block_grads(
            queries,
            segment,
            variate,
            grad_heads,
            log_total,
            row_delta,
            key_rows,
            value_rows,
            key_segs,
            key_vars,
            var_bias,
        )
        query_acc = query_acc + jnp.einsum(
            "htu,uhd->thd", grad_scores, heads_view(key_rows), preferred_element_type=jnp.float32
        )
        key_piece = jnp.einsum(
            "htu,thd->uhd", grad_scores, heads_view(queries), preferred_element_type=jnp.float32
        ).reshape(block_keys, local_width)
        value_piece = jnp.einsum(
            "htu,thd->uhd", probs_low, heads_view(grad_heads), preferred_element_type=jnp.float32
        ).reshape(block_keys, local_width)
        offset = index_block * block_keys
        return (
            (
                query_acc,
                bias_acc + bias_part,
                lax.dynamic_update_slice_in_dim(key_acc, key_piece, offset, 0),
                lax.dynamic_update_slice_in_dim(value_acc, value_piece, offset, 0),
            ),
            None,
        )

    zero_window = jnp.zeros((seq_rows, local_width), jnp.float32)
    (query_acc, bias_acc, key_full, value_full), unused = lax.scan(
        back_pass, (zero_heads, zero_bias, zero_window, zero_window), block_ids
    )
    key_sum, grad_value = (
        lax.psum_scatter(key_full, "dp", scatter_dimension=0, tiled=True),
        lax.psum_scatter(value_full, "dp", scatter_dimension=0, tiled=True),
    )
    grad_key_raw = heads_view(key_sum)
    back_query = rotate_back(query_acc * HD ** (-0.5), cosine, sine_table)
    back_key = rotate_back(grad_key_raw * HD ** (-0.5), cosine, sine_table)
    query_gain_part = jnp.sum(back_query * unit_query, axis=(0, 1))
    key_gain_part = jnp.sum(back_key * unit_key, axis=(0, 1))
    scaled_query = back_query * query_gain
    scaled_key = back_key * key_gain
    grad_raw_query = query_scale * (
        scaled_query - unit_query * jnp.mean(scaled_query * unit_query, axis=-1, keepdims=True)
    )
    grad_raw_key = key_scale * (
        scaled_key - unit_key * jnp.mean(scaled_key * unit_key, axis=-1, keepdims=True)
    )
    grad_projected = jnp.stack(
        [
            grad_raw_query.reshape(tok_rows, local_width),
            grad_raw_key.reshape(tok_rows, local_width),
            grad_value,
        ]
    ).astype(jnp.bfloat16)
    grad_qkv = jnp.einsum(
        "td,kte->kde", normed_one, grad_projected, preferred_element_type=jnp.float32
    )
    grad_normed_one = jnp.einsum(
        "kte,kde->td", grad_projected, w_qkv, preferred_element_type=jnp.float32
    )
    attn_gain_part = jnp.sum(grad_normed_one * unit_one, axis=0)
    scaled_one = grad_normed_one * attn_gain
    input_part = scale_one * (
        scaled_one - unit_one * jnp.mean(scaled_one * unit_one, axis=1, keepdims=True)
    )
    input_share = lax.psum_scatter(input_part, "tensor", scatter_dimension=1, tiled=True)
    grad_input = lax.dynamic_slice_in_dim(grad_middle, tensor_start, width_share, 1) + input_share
    gain_sums = lax.psum(
        (attn_gain_part, mlp_gain_part, query_gain_part, key_gain_part), ("dp", "tensor")
    )
    weight_sums = lax.psum((grad_qkv, grad_out, grad_gateup, grad_down, bias_acc), "dp")
    return (
        output,
        grad_input,
        weight_sums[0],
        weight_sums[1],
        weight_sums[2],
        weight_sums[3],
        gain_sums[0],
        gain_sums[1],
        gain_sums[2],
        gain_sums[3],
        weight_sums[4],
    )


def solution(mesh):
    placed = (
        P("dp", None),
        P("dp", None),
        P("dp"),
        P("dp"),
        P("dp"),
        P(None, None, "tensor"),
        P("tensor", None),
        P(None, None, "tensor"),
        P("tensor", None),
        P(),
        P(),
        P(),
        P(),
        P(None, "tensor"),
    )
    return jax.shard_map(
        shards,
        mesh=mesh,
        in_specs=placed,
        out_specs=(
            P("dp", "tensor"),
            P("dp", "tensor"),
            P(None, None, "tensor"),
            P("tensor", None),
            P(None, None, "tensor"),
            P("tensor", None),
            P(),
            P(),
            P(),
            P(),
            P(None, "tensor"),
        ),
        check_vma=False,
    )
```

profile of v0, /device:TPU:8, one launch (start us, length us, event | category | flops | bytes accessed | tf_op | source)
XLA Modules:
  0.0 1944.2 jit_solution(8415329629730122891)
XLA Ops:
  19.3 19.1 all-gather.1
  38.5 17.7 all-gather.2
  57.9 36.9 %all-gather.7.cloned.1.call-done = bf16[8192,512]{0,1:T(8,128)(2,1)} async-done(((bf16[512,512]{0,1:T(8,128)(2,1)}), bf16[8192,512]{0,1:T(8,128)(2,1)}) %all-gather.7.cloned.1.call-update) | async-done | bytes 8388624 | tf_op jit(solution)/shard_map/all_gather | solution.py:145
  94.9 175.6 %while.43 = (s32[]{:T(128)}, f32[8,512]{1,0:T(8,128)S(1)}, f32[8,512]{1,0:T(8,128)S(1)}, s32[512]{0:T(512)S(1)}, s32[8]{0:T(128)S(1)}, /*index=5*/s32[8192]{0:T(...) while((s32[]{:T(128)}, f32[8,512]{1,0:T(8,128)S(1)}, ...), condition=%wide.region_6.7_spmd.clone, body=%wide.region_3.6_spmd.clone.sunk | while | flops 588271616 | bytes 46903864 | solution.py:177
  98.7 9.2 fusion.131
  107.9 8.9 select_reduce_fusion.2
  120.6 9.2 fusion.131
  129.7 9.2 select_reduce_fusion.2
  142.8 9.2 fusion.131
  151.9 9.1 select_reduce_fusion.2
  164.9 9.1 fusion.131
  174.0 8.9 select_reduce_fusion.2
  186.7 9.2 fusion.131
  195.9 8.9 select_reduce_fusion.2
  208.6 9.2 fusion.131
  217.8 8.9 select_reduce_fusion.2
  230.5 9.2 fusion.131
  239.7 8.9 select_reduce_fusion.2
  252.4 9.2 fusion.131
  261.6 8.9 select_reduce_fusion.2
  270.5 183.1 %while.44 = (s32[]{:T(128)}, f32[512,8,64]{0,2,1:T(8,128)}, f32[512,8,64]{0,2,1:T(8,128)}, s32[8]{0:T(128)S(1)}, bf16[8192,512]{0,1:T(8,128)(2,1)}, /*index=5*/s...) while((s32[]{:T(128)}, f32[512,8,64]{0,2,1:T(8,128)}, ...), condition=%wide.region_8.9_spmd.clone, body=%wide.region_7.8_spmd.clone.sunk | while | flops 1684013056 | bytes 86569592 | solution.py:205
  286.1 6.8 fusion.140
  308.9 6.8 fusion.140
  331.7 6.8 fusion.140
  354.6 6.8 fusion.140
  377.4 6.8 fusion.140
  423.0 6.8 fusion.140
  459.9 63.3 %all-reduce.5.cloned.1.call-done = f32[512,1024]{1,0:T(8,128)} async-done(((f32[512,1024]{1,0:T(8,128)}), f32[512,1024]{1,0:T(8,128)}) %all-reduce.5.cloned.1.call-update) | async-done | bytes 2097168 | tf_op jit(solution)/shard_map/psum | solution.py:209
  542.0 31.9 %reduce-scatter.8.cloned.1.call-done = f32[512,512]{1,0:T(8,128)} async-done(((f32[512,1024]{1,0:T(8,128)}), f32[512,512]{1,0:T(8,128)}) %reduce-scatter.8.cloned.1.call-update) | async-done | bytes 1048592 | tf_op jit(solution)/shard_map/reduce_scatter | solution.py:239
  576.6 33.2 %all-gather.9.cloned.1.call-done = f32[512,1024]{1,0:T(8,128)} async-done(((f32[512,512]{1,0:T(8,128)}), f32[512,1024]{1,0:T(8,128)}) %all-gather.9.cloned.1.call-update) | async-done | bytes 2097168 | tf_op jit(solution)/shard_map/all_gather | solution.py:244
  613.5 7.8 broadcast_in_dim.173
  621.3 7.8 broadcast_in_dim.173.clone
  629.1 394.1 %while.45 = (s32[]{:T(128)}, f32[512,8,64]{0,2,1:T(8,128)}, f32[2,8]{1,0:T(2,128)S(1)}, f32[8192,512]{0,1:T(8,128)}, f32[8192,512]{0,1:T(8,128)}, /*index=5*/s32...) while((s32[]{:T(128)}, f32[512,8,64]{0,2,1:T(8,128)}, ...), condition=%wide.region_18.19_spmd.clone, body=%wide.region_15.18_spmd.clone.sunk | while | flops 2769813504 | bytes 157365424 | solution.py:292
  633.2 8.1 fusion.151
  641.4 14.5 fusion.152
  667.0 9.9 fusion.155
  682.2 8.1 fusion.151
  690.4 14.5 fusion.152
  716.2 9.9 fusion.155
  731.5 8.1 fusion.151
  739.7 14.5 fusion.152
  765.5 9.9 fusion.155
  780.8 8.1 fusion.151
  788.9 14.5 fusion.152
  814.8 9.9 fusion.155
  830.0 8.1 fusion.151
  838.2 14.5 fusion.152
  864.0 9.9 fusion.155
  879.3 8.1 fusion.151
  887.5 14.5 fusion.152
  913.3 9.9 fusion.155
  928.6 8.1 fusion.151
  936.8 14.5 fusion.152
  962.6 9.9 fusion.155
  977.9 8.1 fusion.151
  986.0 14.5 fusion.152
  1011.9 9.9 fusion.155
  1032.5 168.1 %reduce-scatter.10.cloned.1.call-done = f32[512,512]{0,1:T(8,128)} async-done(((f32[8192,512]{0,1:T(8,128)}), f32[512,512]{0,1:T(8,128)}) %reduce-scatter.10.cloned.1.call-update) | async-done | bytes 1048592 | tf_op jit(solution)/shard_map/reduce_scatter | solution.py:296
  1207.2 175.1 %reduce-scatter.12.cloned.1.call-done = f32[512,512]{0,1:T(8,128)} async-done(((f32[8192,512]{0,1:T(8,128)}), f32[512,512]{0,1:T(8,128)}) %reduce-scatter.12.cloned.1.call-update) | async-done | bytes 1048592 | tf_op jit(solution)/shard_map/reduce_scatter | solution.py:297
  1409.1 8.3 reduce-scatter.6.cloned.1.call-done
  1419.8 25.8 %psum.79 = f32[2,8]{1,0:T(2,128)} all-reduce(f32[2,8]{1,0:T(2,128)S(1)} %get-tuple-element.234), channel_id=1, replica_groups=mesh['dp'=16,'tensor'=2] {'dp'}, use_global_device_ids=true, to_apply=%region_39.40 | all-reduce | flops 16 | bytes 128 | tf_op jit(solution)/shard_map/psum | solution.py:335
  1445.8 48.1 %all-reduce = (f32[1024]{0:T(1024)}, f32[1024]{0:T(1024)}, f32[64]{0:T(128)}, f32[64]{0:T(128)}) all-reduce(f32[1024]{0:T(1024)S(1)} %get-tuple-element.404, f32[1024]{0:T(1024)S(1)} %copy-done.64, f32[64]{0:T(128)S(1)} %reduce_sum.173, f32[64]{0:T(128)S(1)} %reduce_sum.176), channel_id=1, replica_groups=mesh['dp'=16,'tensor'=2] {'dp','tensor'}, use_global_device_ids=true, to_apply=%region_30.31 | all-reduce | flops 2176 | bytes 17408 | tf_op jit(solution)/shard_map/psum | solution.py:332
  1496.6 412.7 %all-reduce.7.cloned.1.call-done = (f32[3,1024,512]{1,2,0:T(8,128)}, f32[512,1024]{1,0:T(8,128)}, f32[2,1024,1408]{1,2,0:T(8,128)}, f32[1408,1024]{1,0:T(8,128)}) async-done(((f32[3,1024,512]{1,2,0:T(8,128)}, f32[512,1024]{1,0:T(8,128)}, f32[2,1024,1408]{1,2,0:T(8,128)}, f32[1408,1024]{1,0:T(8,128)}), (f32[3,1024,512]{1,2,0:T(8,128)}, f32[512,1024]{1,0:T(8,128)}, f32[2,1024,1408]{1,2,0:T(8,128)}, ...) | async-done | bytes 25690128 | tf_op jit(solution)/shard_map/psum | solution.py:335
  1915.9 11.9 copy.54
  (714 shorter events, 395.9 us)
Async XLA Ops:
  7.2 87.7 %all-gather.7.cloned.1.call-start = ((), (), s32[]{:S(2)}) async-start(), calls=%async_computation.5 | async-start | bytes 8912896 | tf_op jit(solution)/shard_map/all_gather | solution.py:145
  15.1 23.4 %copy-start.40 = (s32[512]{0:T(512)S(1)}, s32[512]{0:T(512)}, u32[]{:S(2)}) copy-start(s32[512]{0:T(512)} %param.23) | copy-start | bytes 6148
  15.1 79.7 %copy-start.52 = (f32[2,8]{1,0:T(2,128)S(1)}, f32[2,8]{1,0:T(2,128)}, u32[]{:S(2)}) copy-start(f32[2,8]{1,0:T(2,128)} %param.33) | copy-start | bytes 196
  17.1 253.4 %all-gather.11.cloned.1.call-start = ((), (), s32[]{:S(2)}) async-start(), calls=%async_computation.13 | async-start | bytes 8912896 | tf_op jit(solution)/shard_map/all_gather | solution.py:146
  19.2 504.0 %all-reduce.5.cloned.1.call-start = ((), (), s32[]{:S(2)}) async-start(), calls=%async_computation.6 | async-start | bytes 4194304 | tf_op jit(solution)/shard_map/psum | solution.py:209
  97.0 10.9 copy-start.6
  97.0 10.9 copy-start.7
  118.9 10.9 copy-start.6
  118.9 10.9 copy-start.7
  141.1 10.9 copy-start.6
  141.1 10.9 copy-start.7
  163.2 10.9 copy-start.6
  163.2 10.8 copy-start.7
  185.0 10.9 copy-start.6
  185.0 10.9 copy-start.7
  206.9 10.9 copy-start.6
  206.9 10.9 copy-start.7
  228.8 10.9 copy-start.6
  228.8 10.9 copy-start.7
  250.7 10.9 copy-start.6
  250.7 10.9 copy-start.7
  459.7 65.8 %copy-start.55 = (f32[1024]{0:T(1024)S(1)}, f32[1024]{0:T(1024)}, u32[]{:S(2)}) copy-start(f32[1024]{0:T(1024)} %param.30) | copy-start | bytes 12292
  459.7 114.3 %reduce-scatter.8.cloned.1.call-start = ((), (), s32[]{:S(2)}) async-start(), calls=%async_computation.8 | async-start | bytes 3145728 | tf_op jit(solution)/shard_map/reduce_scatter | solution.py:239
  525.5 14.7 copy-start.9
  525.5 14.7 copy-start.53
  525.5 10.6 slice-start
  542.0 67.8 %all-gather.9.cloned.1.call-start = ((), (), s32[]{:S(2)}) async-start(), calls=%async_computation.9 | async-start | bytes 3145728 | tf_op jit(solution)/shard_map/all_gather | solution.py:244
  576.5 624.1 %reduce-scatter.10.cloned.1.call-start = ((), (), s32[]{:S(2)}) async-start(), calls=%async_computation.10 | async-start | bytes 17825792 | tf_op jit(solution)/shard_map/reduce_scatter | solution.py:296
  632.3 9.0 copy-start.2
  633.2 8.2 copy-start.16
  633.2 8.2 copy-start.18
  633.2 8.2 copy-start.41
  681.3 9.0 copy-start.2
  682.2 8.2 copy-start.16
  682.2 8.2 copy-start.18
  730.6 9.0 copy-start.2
  731.5 8.2 copy-start.16
  731.5 8.2 copy-start.18
  779.9 9.0 copy-start.2
  780.7 8.2 copy-start.16
  780.7 8.2 copy-start.18
  829.1 9.0 copy-start.2
  830.0 8.2 copy-start.16
  830.0 8.2 copy-start.18
  830.0 8.2 copy-start.41
  878.4 9.0 copy-start.2
  879.3 8.2 copy-start.16
  879.3 8.2 copy-start.18
  927.7 9.0 copy-start.2
  928.5 8.2 copy-start.16
  928.6 8.2 copy-start.18
  977.0 9.0 copy-start.2
  977.8 8.2 copy-start.16
  977.8 8.2 copy-start.18
  1023.2 359.1 %reduce-scatter.12.cloned.1.call-start = ((), (), s32[]{:S(2)}) async-start(), calls=%async_computation.11 | async-start | bytes 17825792 | tf_op jit(solution)/shard_map/reduce_scatter | solution.py:297
  1024.0 393.4 %reduce-scatter.6.cloned.1.call-start = ((), (), s32[]{:S(2)}) async-start(), calls=%async_computation.7 | async-start | bytes 3145728 | tf_op jit(solution)/shard_map/reduce_scatter | solution.py:221
  1029.8 172.2 %copy-start.36 = (f32[512,32]{0,1:T(8,128)S(1)}, f32[512,32]{0,1:T(8,128)}, u32[]{:S(2)}) copy-start(f32[512,32]{0,1:T(8,128)} %copy-done.35) | copy-start | bytes 196612
  1029.8 172.2 %copy-start.38 = (f32[512,32]{0,1:T(8,128)S(1)}, f32[512,32]{0,1:T(8,128)}, u32[]{:S(2)}) copy-start(f32[512,32]{0,1:T(8,128)} %copy-done.37) | copy-start | bytes 196612
  1029.9 464.0 %reduce-scatter.14.cloned.1.call-start = ((), (), s32[]{:S(2)}) async-start(), calls=%async_computation.12 | async-start | bytes 3145728 | tf_op jit(solution)/shard_map/reduce_scatter | solution.py:330
  1032.5 171.2 %copy-start.48 = (f32[512,8]{0,1:T(8,128)S(1)}, f32[512,8]{0,1:T(8,128)}, u32[]{:S(2)}) copy-start(f32[512,8]{0,1:T(8,128)} %copy-done.47) | copy-start | bytes 49156
  1205.5 178.1 %copy-start.58 = (f32[512]{0:T(512)S(1)}, f32[512]{0:T(512)}, u32[]{:S(2)}) copy-start(f32[512]{0:T(512)} %copy-done.57) | copy-start | bytes 6148
  1205.5 178.1 %copy-start.63 = (f32[1024]{0:T(1024)S(1)}, f32[1024]{0:T(1024)}, u32[]{:S(2)}) copy-start(f32[1024]{0:T(1024)} %param.29) | copy-start | bytes 12292
  1389.6 519.7 %all-reduce.7.cloned.1.call-start = ((), (), s32[]{:S(2)}) async-start(), calls=%async_computation.14 | async-start | bytes 51380224 | tf_op jit(solution)/shard_map/psum | solution.py:335
  1409.0 36.8 %copy-start.64 = (f32[1024]{0:T(1024)S(1)}, f32[1024]{0:T(1024)}, u32[]{:S(2)}) copy-start(f32[1024]{0:T(1024)} %get-tuple-element.402) | copy-start | bytes 12292
  (141 other events, 562.6 us)
Sparse Core Ops, SparseCore 0:
  17.2 77.6 all-gather.6
  97.6 76.2 all-gather.10
  459.8 63.3 all-reduce.4
  542.1 31.8 reduce-scatter.7
  576.6 33.1 all-gather.8
  1023.4 177.1 reduce-scatter.9
  1204.7 177.5 reduce-scatter.11
  1385.1 32.2 reduce-scatter.5
  1419.7 31.8 reduce-scatter.13
  1456.8 452.5 all-reduce.6
where the time goes:
time: 1960 us; the launch traced here: 1940 us
  waiting for transfers between devices  931 us (48%)
  matrix products  592 us (30%)
  local copies, waits for them, and re-layouts  152 us (8%)
  other arithmetic  123 us (6%)
  blocking collectives  111 us (6%)
    psum x1, waiting for transfers between devices, shards(): lax.psum((grad_qkv, grad_out, grad_gateup, grad_down, bias_acc), 'dp')  413 us
    reduce_scatter x1, waiting for transfers between devices, shards(): lax.psum_scatter(value_full, 'dp', scatter_dimension=0, tiled=True)  175 us
    dot_general x24, matrix products, block_scores(): jnp.einsum('thd,uhd->htu', heads_view(query_rows), heads_view(key_rows),...  169 us
    reduce_scatter x1, waiting for transfers between devices, shards(): lax.psum_scatter(key_full, 'dp', scatter_dimension=0, tiled=True)  168 us
    dot_general x8, matrix products, block_grads(): jnp.einsum('thd,uhd->htu', heads_view(grad_rows), heads_view(value_rows),...  116 us
    dot_general x8, matrix products, back_pass(): jnp.einsum('htu,thd->uhd', probs_low, heads_view(grad_heads), preferred_e...  79.3 us
    reduce_sum x8, other arithmetic, first_pass(): jnp.sum(kept_terms, axis=2)  71.4 us
    psum x1, waiting for transfers between devices, shards(): attn_total = lax.psum(attn_part, 'tensor')  63.3 us
  transfers between devices with their start and end apart: 10, of which 8 were waited for; matrix products, arithmetic and copies ran while one was open for 11% of the time, Pallas kernels for 0%

commit v1 on v0

v1 whole, which is shorter than its diff:
```python
import functools

import jax
import jax.numpy as jnp
from jax import lax
from jax.experimental import pallas as pl
from jax.experimental.pallas import tpu as pltpu
from jax.sharding import PartitionSpec as P

HD = 64
LANES = 128
EPSILON = 1e-05
LOG2E = 1.4426950408889634
FAR = -30000.0
DOCS = 8
VARS = 4
VAR_AT = HD
SEG_AT = VAR_AT + 3 * VARS
ONE_AT = SEG_AT + DOCS
VMEM = 60 * 1024 * 1024


def heads_view(rows):
    return rows.reshape(rows.shape[0], -1, HD)


def rotary_table(times):
    half_dim = HD // 2
    inverse = 10000.0 ** (-2.0 * jnp.arange(half_dim, dtype=jnp.float32) / HD)
    angles = times.astype(jnp.float32)[:, None] * inverse[None, :]
    return (jnp.cos(angles)[:, None, :], jnp.sin(angles)[:, None, :])


def rotate(values, cosine, sine_table):
    half_dim = values.shape[-1] // 2
    first_half = values[..., :half_dim]
    second_half = values[..., half_dim:]
    return jnp.concatenate(
        [
            first_half * cosine - second_half * sine_table,
            second_half * cosine + first_half * sine_table,
        ],
        axis=-1,
    )


def rotate_back(grads_in, cosine, sine_table):
    return rotate(grads_in, cosine, -sine_table)


def split_three(x):
    high = lax.reduce_precision(x, 8, 7)
    rest = x - high
    mid = lax.reduce_precision(rest, 8, 7)
    return [part.astype(jnp.bfloat16) for part in (high, mid, rest - mid)]


def forward_kernel(lo_ref, hi_ref, q_ref, k_ref, v_ref, o_ref, acc_ref, *, rows, ranks, heads):
    block = pl.program_id(0)
    acc_ref[...] = jnp.zeros_like(acc_ref)
    query = q_ref[...]

    def step(index, carry):
        place = lax.rem(index, ranks) * heads + index // ranks
        span = pl.ds(pl.multiple_of(place * rows, rows), rows)
        scores = lax.dot_general(
            query, k_ref[span, :], (((1,), (1,)), ((), ())), preferred_element_type=jnp.float32
        )
        probs = jnp.exp2(scores).astype(jnp.bfloat16)
        acc_ref[...] += jnp.dot(probs, v_ref[span, :], preferred_element_type=jnp.float32)
        return carry

    lax.fori_loop(lo_ref[block], hi_ref[block], step, 0)
    total = acc_ref[...]
    row_sum = total[:, HD : HD + 1]
    lane = lax.broadcasted_iota(jnp.int32, total.shape, 1)
    o_ref[...] = jnp.where(lane < HD, total / row_sum, jnp.log2(row_sum))


def forward_attention(lo, hi, query, key, value, rows, ranks, heads):
    blocks = query.shape[0] // rows
    whole = pl.BlockSpec(memory_space=pltpu.VMEM)
    return pl.pallas_call(
        functools.partial(forward_kernel, rows=rows, ranks=ranks, heads=heads),
        out_shape=jax.ShapeDtypeStruct(query.shape, jnp.float32),
        grid_spec=pltpu.PrefetchScalarGridSpec(
            num_scalar_prefetch=2,
            grid=(blocks,),
            in_specs=[pl.BlockSpec((rows, LANES), lambda i, *_: (i, 0)), whole, whole],
            out_specs=pl.BlockSpec((rows, LANES), lambda i, *_: (i, 0)),
            scratch_shapes=[pltpu.VMEM((rows, LANES), jnp.float32)],
        ),
        compiler_params=pltpu.CompilerParams(vmem_limit_bytes=VMEM),
    )(lo, hi, query, key, value)


def backward_kernel(
    lo_ref, hi_ref, k_ref, v_ref, q_ref, g_ref, dk_ref, dv_ref, dq_ref, *, rows
):
    @pl.when(pl.program_id(0) == 0)
    def start():
        dq_ref[...] = jnp.zeros_like(dq_ref)

    dk_ref[...] = jnp.zeros_like(dk_ref)
    dv_ref[...] = jnp.zeros_like(dv_ref)
    key = k_ref[...]
    value = v_ref[...]

    def step(index, carry):
        span = pl.ds(pl.multiple_of(index * rows, rows), rows)
        query = q_ref[span, :]
        grad = g_ref[span, :]
        scores = lax.dot_general(
            key, query, (((1,), (1,)), ((), ())), preferred_element_type=jnp.float32
        )
        grad_probs = lax.dot_general(
            value, grad, (((1,), (1,)), ((), ())), preferred_element_type=jnp.float32
        )
        probs = jnp.exp2(scores)
        grad_scores = (probs * grad_probs).astype(jnp.bfloat16)
        dv_ref[...] += jnp.dot(
            probs.astype(jnp.bfloat16), grad, preferred_element_type=jnp.float32
        )
        dk_ref[...] += jnp.dot(grad_scores, query, preferred_element_type=jnp.float32)
        dq_ref[span, :] += lax.dot_general(
            grad_scores, key, (((0,), (0,)), ((), ())), preferred_element_type=jnp.float32
        )
        return carry

    block = pl.program_id(0)
    lax.fori_loop(lo_ref[block], hi_ref[block], step, 0)


def backward_attention(lo, hi, key, value, query, grad, rows, ranks, heads):
    blocks = key.shape[0] // rows
    whole = pl.BlockSpec(memory_space=pltpu.VMEM)

    part = pl.BlockSpec((rows, LANES), lambda i, *_: (i, 0))
    return pl.pallas_call(
        functools.partial(backward_kernel, rows=rows),
        out_shape=(
            jax.ShapeDtypeStruct(key.shape, jnp.float32),
            jax.ShapeDtypeStruct(key.shape, jnp.float32),
            jax.ShapeDtypeStruct(query.shape, jnp.float32),
        ),
        grid_spec=pltpu.PrefetchScalarGridSpec(
            num_scalar_prefetch=2,
            grid=(blocks,),
            in_specs=[part, part, whole, whole],
            out_specs=(part, part, whole),
            scratch_shapes=[],
        ),
        compiler_params=pltpu.CompilerParams(vmem_limit_bytes=VMEM),
    )(lo, hi, key, value, query, grad)


def shards(
    tokens,
    cotangent,
    segment,
    variate,
    time,
    w_qkv,
    w_out,
    w_gateup,
    w_down,
    attn_gain,
    mlp_gain,
    query_gain,
    key_gain,
    var_bias,
):
    low = jnp.bfloat16
    wide = jnp.float32
    rows = tokens.shape[0]
    local_width = w_qkv.shape[2]
    heads = local_width // HD
    dp = lax.axis_size("dp")
    tensor = lax.axis_size("tensor")
    ranks = dp // heads
    head_groups = [[h * ranks + j for h in range(heads)] for j in range(ranks)]
    rank_groups = [[h * ranks + j for j in range(ranks)] for h in range(heads)]
    place = lax.axis_index("dp")
    head_here = place // ranks
    rank_here = lax.rem(place, ranks)
    width_share = tokens.shape[1] // tensor
    tensor_start = lax.axis_index("tensor") * width_share

    def to_heads(x):
        return lax.all_to_all(x, "dp", 0, 0, axis_index_groups=head_groups, tiled=True)

    def tensor_sum(x):
        if tensor == 2:
            return x + lax.ppermute(x.astype(low), "tensor", [(0, 1), (1, 0)]).astype(wide)
        return lax.psum(x.astype(low), "tensor").astype(wide)

    def tensor_share(x):
        mine = lax.dynamic_slice_in_dim(x, tensor_start, width_share, 1)
        if tensor == 2:
            other = lax.dynamic_slice_in_dim(x, width_share - tensor_start, width_share, 1)
            return mine + lax.ppermute(other.astype(low), "tensor", [(0, 1), (1, 0)]).astype(wide)
        return lax.psum_scatter(x, "tensor", scatter_dimension=1, tiled=True)

    inputs = tokens.astype(wide)
    scale_one = lax.rsqrt(jnp.mean(inputs * inputs, axis=1, keepdims=True) + EPSILON)
    unit_one = inputs * scale_one
    normed_one = (unit_one * attn_gain).astype(low)
    projected = jnp.einsum("td,kde->kte", normed_one, w_qkv, preferred_element_type=wide)
    cosine, sine_table = rotary_table(time)
    raw_query = heads_view(projected[0])
    raw_key = heads_view(projected[1])
    query_scale = lax.rsqrt(jnp.mean(raw_query * raw_query, axis=-1, keepdims=True) + EPSILON)
    key_scale = lax.rsqrt(jnp.mean(raw_key * raw_key, axis=-1, keepdims=True) + EPSILON)
    unit_query = raw_query * query_scale
    unit_key = raw_key * key_scale
    query_rows = rotate(unit_query * (query_gain * (LOG2E * HD**-0.5)), cosine, sine_table)
    key_rows = rotate(unit_key * key_gain, cosine, sine_table)
    packed = jnp.concatenate(
        [query_rows.astype(low), key_rows.astype(low), heads_view(projected[2]).astype(low)], axis=-1
    ).transpose(1, 0, 2)
    all_ids = lax.all_gather(jnp.stack([segment, variate]), "dp", axis=0, tiled=False)
    landed = to_heads(packed)
    gathered = lax.all_gather(
        landed[:, :, HD:], "dp", axis=0, axis_index_groups=rank_groups, tiled=False
    )

    ids = all_ids.reshape(heads, ranks, 2, rows).transpose(1, 0, 2, 3)
    segs = ids[:, :, 0]
    variates = ids[:, :, 1]
    own_segs = lax.dynamic_index_in_dim(segs, rank_here, 0, False)
    own_vars = lax.dynamic_index_in_dim(variates, rank_here, 0, False)
    all_rows = dp * rows
    own_rows = heads * rows

    def hot(values, count):
        return values.reshape(-1, 1) == jnp.arange(count, dtype=jnp.int32)[None, :]

    bias_here = lax.dynamic_index_in_dim(var_bias, head_here, 1, False)
    bias_step = split_three(jnp.broadcast_to((bias_here[0] - bias_here[1]) * LOG2E, (1, 1)))
    own_hot = hot(own_vars, VARS)
    query_head = landed[:, :, :HD].reshape(own_rows, HD)
    query_features = [jnp.where(own_hot, part, 0).astype(low) for part in bias_step] + [
        hot(own_segs, DOCS).astype(low)
    ]
    fill = jnp.zeros((own_rows, LANES - ONE_AT), low)
    query_op = jnp.concatenate([query_head] + query_features + [fill], axis=1)
    key_hot = hot(variates, VARS).astype(low)
    key_op = jnp.concatenate(
        [
            gathered[..., :HD].reshape(all_rows, HD),
            key_hot,
            key_hot,
            key_hot,
            jnp.where(hot(segs, DOCS), 0.0, FAR).astype(low),
            jnp.ones((all_rows, 3), low),
            jnp.zeros((all_rows, LANES - ONE_AT - 3), low),
        ],
        axis=1,
    )
    value_op = jnp.concatenate(
        [
            gathered[..., HD:].reshape(all_rows, HD),
            jnp.ones((all_rows, 3), low),
            jnp.zeros((all_rows, LANES - HD - 3), low),
        ],
        axis=1,
    )
    block_first = all_ids[:, 0, 0]
    block_last = all_ids[:, 0, -1]
    own_first = own_segs[:, 0]
    own_last = own_segs[:, -1]
    count = lambda hits, axis: jnp.sum(hits.astype(jnp.int32), axis=axis)
    key_lo = count(block_last[None, :] < own_first[:, None], 1)
    key_hi = count(block_first[None, :] <= own_last[:, None], 1)
    place_first = segs[:, :, 0].reshape(-1)
    place_last = segs[:, :, -1].reshape(-1)
    query_lo = count(own_last[None, :] < place_first[:, None], 1)
    query_hi = count(own_first[None, :] <= place_last[:, None], 1)

    mixed = forward_attention(key_lo, key_hi, query_op, key_op, value_op, rows, ranks, heads)
    exact_out = mixed[:, :HD]
    log_total = mixed[:, HD : HD + 1]

    def to_tokens(x):
        return lax.all_to_all(x, "dp", 0, 0, axis_index_groups=head_groups, tiled=True)

    heads_out = (
        to_tokens(exact_out.astype(low).reshape(heads, rows, HD))
        .transpose(1, 0, 2)
        .reshape(rows, local_width)
    )
    attn_total = tensor_sum(jnp.dot(heads_out, w_out, preferred_element_type=wide))
    middle = inputs + attn_total
    scale_two = lax.rsqrt(jnp.mean(middle * middle, axis=1, keepdims=True) + EPSILON)
    unit_two = middle * scale_two
    normed_two = (unit_two * mlp_gain).astype(low)
    gate_up = jnp.einsum("td,kdf->ktf", normed_two, w_gateup, preferred_element_type=wide)
    gate_vals = gate_up[0]
    up_vals = gate_up[1]
    sig_gate = jax.nn.sigmoid(gate_vals)
    act_gate = gate_vals * sig_gate
    hidden = (act_gate * up_vals).astype(low)
    mlp_part = jnp.dot(hidden, w_down, preferred_element_type=wide)
    mlp_share = tensor_share(mlp_part)
    output = (lax.dynamic_slice_in_dim(middle, tensor_start, width_share, 1) + mlp_share).astype(low)
    grad_hidden = jnp.einsum("te,fe->tf", cotangent, w_down, preferred_element_type=wide)
    grad_down = jnp.einsum("tf,te->fe", hidden, cotangent, preferred_element_type=wide)
    grad_gate = grad_hidden * up_vals * sig_gate * (1.0 + gate_vals * (1.0 - sig_gate))
    grad_up = grad_hidden * act_gate
    grad_gu = jnp.stack([grad_gate, grad_up]).astype(low)
    grad_gateup = jnp.einsum("td,ktf->kdf", normed_two, grad_gu, preferred_element_type=wide)
    grad_normed_two = jnp.einsum("ktf,kdf->td", grad_gu, w_gateup, preferred_element_type=wide)
    mlp_gain_part = jnp.sum(grad_normed_two * unit_two, axis=0)
    scaled_two = grad_normed_two * mlp_gain
    middle_part = scale_two * (
        scaled_two - unit_two * jnp.mean(scaled_two * unit_two, axis=1, keepdims=True)
    )
    grad_middle = cotangent.astype(wide) + tensor_sum(middle_part)
    grad_middle_low = grad_middle.astype(low)
    grad_out = jnp.einsum("tc,td->cd", heads_out, grad_middle_low, preferred_element_type=wide)
    grad_heads = jnp.einsum(
        "td,cd->tc", grad_middle_low, w_out, preferred_element_type=wide
    ).astype(low)
    grad_landed = to_heads(heads_view(grad_heads).transpose(1, 0, 2)).reshape(own_rows, HD)
    row_delta = jnp.sum(grad_landed.astype(wide) * exact_out, axis=1, keepdims=True)
    grad_op = jnp.concatenate(
        [grad_landed] + split_three(-row_delta) + [jnp.zeros((own_rows, LANES - HD - 3), low)],
        axis=1,
    )
    query_back = jnp.concatenate(
        [query_op[:, :ONE_AT]]
        + split_three(-log_total)
        + [jnp.zeros((own_rows, LANES - ONE_AT - 3), low)],
        axis=1,
    )
    key_full, value_full, query_full = backward_attention(
        query_lo, query_hi, key_op, value_op, query_back, grad_op, rows, ranks, heads
    )
    by_variate = query_full[:, VAR_AT : VAR_AT + VARS]
    same_sum = jnp.sum(jnp.where(own_hot, by_variate, 0.0))
    other_sum = jnp.sum(jnp.where(own_hot, 0.0, by_variate))
    bias_part = jnp.stack([same_sum, other_sum])[:, None] * (
        jnp.arange(heads, dtype=jnp.int32)[None, :] == head_here
    ).astype(wide)

    key_value = jnp.concatenate([key_full[:, :HD], value_full[:, :HD]], axis=1).astype(low)
    key_value = lax.psum_scatter(
        key_value.reshape(ranks, heads, rows, 2 * HD),
        "dp",
        scatter_dimension=0,
        axis_index_groups=rank_groups,
        tiled=False,
    )
    back_packed = jnp.concatenate(
        [query_full[:, :HD].astype(low).reshape(heads, rows, HD), key_value], axis=-1
    )
    back_landed = to_tokens(back_packed).transpose(1, 0, 2).astype(wide)
    back_query = rotate_back(back_landed[..., :HD] * HD ** (-0.5), cosine, sine_table)
    back_key = rotate_back(back_landed[..., HD : 2 * HD] * (1.0 / LOG2E), cosine, sine_table)
    grad_value = back_landed[..., 2 * HD :].reshape(rows, local_width)
    query_gain_part = jnp.sum(back_query * unit_query, axis=(0, 1))
    key_gain_part = jnp.sum(back_key * unit_key, axis=(0, 1))
    scaled_query = back_query * query_gain
    scaled_key = back_key * key_gain
    grad_raw_query = query_scale * (
        scaled_query - unit_query * jnp.mean(scaled_query * unit_query, axis=-1, keepdims=True)
    )
    grad_raw_key = key_scale * (
        scaled_key - unit_key * jnp.mean(scaled_key * unit_key, axis=-1, keepdims=True)
    )
    grad_projected = jnp.stack(
        [
            grad_raw_query.reshape(rows, local_width),
            grad_raw_key.reshape(rows, local_width),
            grad_value,
        ]
    ).astype(low)
    grad_qkv = jnp.einsum("td,kte->kde", normed_one, grad_projected, preferred_element_type=wide)
    grad_normed_one = jnp.einsum("kte,kde->td", grad_projected, w_qkv, preferred_element_type=wide)
    attn_gain_part = jnp.sum(grad_normed_one * unit_one, axis=0)
    scaled_one = grad_normed_one * attn_gain
    input_part = scale_one * (
        scaled_one - unit_one * jnp.mean(scaled_one * unit_one, axis=1, keepdims=True)
    )
    grad_input = lax.dynamic_slice_in_dim(grad_middle, tensor_start, width_share, 1) + tensor_share(
        input_part
    )
    gain_sums = lax.psum(
        (attn_gain_part, mlp_gain_part, query_gain_part, key_gain_part), ("dp", "tensor")
    )
    bias_sum = lax.psum(bias_part, "dp")
    early = lax.psum((grad_out.astype(low), grad_gateup.astype(low), grad_down.astype(low)), "dp")
    late = lax.psum(grad_qkv.astype(low), "dp")
    return (
        output,
        grad_input,
        late.astype(wide),
        early[0].astype(wide),
        early[1].astype(wide),
        early[2].astype(wide),
        gain_sums[0],
        gain_sums[1],
        gain_sums[2],
        gain_sums[3],
        bias_sum,
    )


def solution(mesh):
    placed = (
        P("dp", None),
        P("dp", None),
        P("dp"),
        P("dp"),
        P("dp"),
        P(None, None, "tensor"),
        P("tensor", None),
        P(None, None, "tensor"),
        P("tensor", None),
        P(),
        P(),
        P(),
        P(),
        P(None, "tensor"),
    )
    return jax.shard_map(
        shards,
        mesh=mesh,
        in_specs=placed,
        out_specs=(
            P("dp", "tensor"),
            P("dp", "tensor"),
            P(None, None, "tensor"),
            P("tensor", None),
            P(None, None, "tensor"),
            P("tensor", None),
            P(),
            P(),
            P(),
            P(),
            P(None, "tensor"),
        ),
        check_vma=False,
    )
```

time: 1960 us -> 747 us (0.38)
  waiting for transfers between devices: 931 us -> 209 us
  matrix products: 592 us -> 43.2 us
  Pallas kernels: 0 us -> 135 us
  other arithmetic: 123 us -> 64.7 us
  local copies, waits for them, and re-layouts: 152 us -> 116 us
  starting transfers between devices: 1.16 us -> 23.1 us
    dot_general x82 -> x10, matrix products: 585 us -> 37.8 us  [the longest x1 6.45 us: shards(): jnp.einsum('td,kdf->ktf', normed_two, w_gateup, preferred_element_type=wide)]
    reduce_scatter x5 -> x1, waiting for transfers between devices: 383 us -> 5.91 us  [shards(): lax.psum_scatter(key_value.reshape(ranks, heads, rows, 2 * HD), 'dp', sca...]
    psum x2 -> x1, waiting for transfers between devices: 476 us -> 144 us  [shards(): late = lax.psum(grad_qkv.astype(low), 'dp')]
    pallas_call x0 -> x2, Pallas kernels: none -> 135 us  [the longest x1 86.6 us: backward_attention(): pl.pallas_call(functools.partial(backward_kernel, rows=rows), out_shape=(...]
    all_gather x3 -> x1, waiting for transfers between devices: 70.2 us -> 0.01 us  [shards(): lax.all_gather(landed[:, :, HD:], 'dp', axis=0, axis_index_groups=rank_gr...]
    dynamic_slice x96 -> x3, local copies, waits for them, and re-layouts: 66.4 us -> 0.1 us  [the longest x1 0.07 us: shards(): bias_here = lax.dynamic_index_in_dim(var_bias, head_here, 1, False)]
    reduce_sum x8 -> x4, other arithmetic: 71.4 us -> 6.27 us  [the longest x1 2.47 us: shards(): jnp.sum(grad_landed.astype(wide) * exact_out, axis=1, keepdims=True)]
    concatenate x0 -> x8, local copies, waits for them, and re-layouts: none -> 43.7 us  [the longest x1 14.3 us: shards(): jnp.concatenate([gathered[..., :HD].reshape(all_rows, HD), key_hot, key_h...]
  transfers between devices with their start and end apart: 10 -> 10, of which waited for: 8 -> 6; matrix products, arithmetic and copies ran while one was open for 11% -> 11% of each run, Pallas kernels for 0% -> 0%
where the time goes in v1:
time: 747 us; the launch traced here: 739 us
  waiting for transfers between devices  209 us (28%)
  Pallas kernels  135 us (18%)
  blocking collectives  128 us (17%)
  local copies, waits for them, and re-layouts  116 us (16%)
  other arithmetic  64.7 us (9%)
  matrix products  43.2 us (6%)
  starting transfers between devices  23.1 us (3%)
  between operations  19.7 us (3%)
    psum x1, waiting for transfers between devices, shards(): late = lax.psum(grad_qkv.astype(low), 'dp')  144 us
    pallas_call x1, Pallas kernels, backward_attention(): pl.pallas_call(functools.partial(backward_kernel, rows=rows), out_shape=(...  86.6 us
    pallas_call x1, Pallas kernels, forward_attention(): pl.pallas_call(functools.partial(forward_kernel, rows=rows, ranks=ranks,...  48.4 us
    psum x1, blocking collectives, shards(): lax.psum((attn_gain_part, mlp_gain_part, query_gain_part, key_gain_part),...  48.4 us
    all_gather x1, blocking collectives, shards(): lax.all_gather(jnp.stack([segment, variate]), 'dp', axis=0, tiled=False)  40 us
    ppermute x2, waiting for transfers between devices, tensor_sum(): lax.ppermute(x.astype(low), 'tensor', [(0, 1), (1, 0)]).astype(wide)  32.5 us
    psum x1, blocking collectives, shards(): bias_sum = lax.psum(bias_part, 'dp')  25.9 us
    unnamed x97, local copies, waits for them, and re-layouts  23.8 us
  transfers between devices with their start and end apart: 10, of which 6 were waited for; matrix products, arithmetic and copies ran while one was open for 11% of the time, Pallas kernels for 0%

profile of v1, /device:TPU:8, one launch (start us, length us, event | category | flops | bytes accessed | tf_op | source)
XLA Modules:
  0.0 738.6 jit_solution(13244942614168069496)
XLA Ops:
  9.4 3.1 convolution_bitcast_fusion.1
  17.2 6.3 all-to-all-start
  29.0 40.0 %all-gather.2 = s32[16,2,512]{2,1,0:T(2,128)S(1)} all-gather(s32[1,2,512]{2,1,0:T(2,128)S(1)} %add_bitcast_fusion), channel_id=2, replica_groups=mesh['dp'=16,'tensor'=2] {'dp'}, dimensions={0}, use_global_device_ids=true | all-gather | bytes 69632 | tf_op jit(solution)/shard_map/all_gather | solution.py:221
  69.2 3.2 fusion.15
  72.5 2.7 fusion.18
  75.1 4.6 fusion
  79.8 2.3 slice.167
  82.0 2.3 copy.140
  86.0 4.6 select_convert_fusion
  90.6 1.9 slice.165
  92.6 2.4 copy.139
  96.0 7.3 concatenate.48.q_ref
  103.4 4.4 fusion.48
  108.0 2.6 maximum_maximum_fusion.v_ref
  112.3 14.3 %concatenate.49.k_ref = bf16[8192,128]{1,0:T(8,128)(2,1)} concatenate(bf16[8192,64]{1,0:T(8,128)(2,1)} %bitcast.188, bf16[8192,4]{1,0:T(8,128)(2,1)} %fusion, bf16[8192,4]{1,0:T(8,128)(2,1)} %fusion, bf16[8192,4]{1,0:T(8,128)(2,1)} %fusion, bf16[8192,8]{1,0:T(8,128)(2,1)} %select_convert_fusion, bf16[8192,3]{1,0:T(8,128)(2,1)} %copy-done.6, bf16[8192,41]{1,0:T(8,128)(2,1)} %broadcast_in_dim.97), dimensions={1} | concatenate | bytes 4194304 | tf_op jit(solution)/shard_map/concatenate | solution.py:248
  126.6 48.4 %shard_map.221 = f32[4096,128]{1,0:T(8,128)} custom-call(s32[8]{0:T(128)} %get-tuple-element.161.lo_ref, s32[8]{0:T(128)} %get-tuple-element.160.hi_ref, bf16[4096,128]{1,0:T(8,128)(2,1)} %concatenate.48.q_ref, bf16[8192,128]{1,0:T(8,128)(2,1)} %concatenate.49.k_ref, bf16[8192,128]{1,0:T(8,128)(2,1)} %maximum_maximum_fusion.v_ref), custom_call_target="tpu_custom_call" | custom-call | tf_op jit(solution)/shard_map/pallas_call | solution.py:83
  175.0 2.7 slice.266
  177.6 2.3 copy.143
  180.0 13.9 %all_to_all.20 = bf16[8,512,64]{1,2,0:T(8,128)(2,1)S(1)} all-to-all(bf16[8,512,64]{1,2,0:T(8,128)(2,1)} %copy.143), channel_id=1, replica_groups={{0,4,8,12,16,20,24,28},{2,6,10,14,18,22,26,30},{1,5,9,13,17,21,25,29},{..., dimensions={0} | all-to-all | bytes 1048576 | tf_op jit(solution)/shard_map/all_to_all | solution.py:285
  193.8 2.2 fusion.53
  197.6 17.1 %collective-permute-done = bf16[512,1024]{1,0:T(8,128)(2,1)S(1)} collective-permute-done((bf16[512,1024]{1,0:T(8,128)(2,1)S(1)}, bf16[512,1024]{1,0:T(8,128)(2,1)S(1)}, u32[]{:S(2)}, u32[]{:S(2)}) %collective-permute-start) | collective-permute-done | bytes 1048608 | tf_op jit(solution)/shard_map/ppermute | solution.py:194
  215.4 6.4 convolution_bitcast_fusion
  221.9 4.0 fusion.21
  225.9 3.4 fusion.14
  233.6 15.4 %collective-permute-done.2 = bf16[512,1024]{1,0:T(8,128)(2,1)} collective-permute-done((bf16[512,1024]{1,0:T(8,128)(2,1)}, bf16[512,1024]{1,0:T(8,128)(2,1)}, u32[]{:S(2)}, u32[]{:S(2)}) %collective-permute-start.2) | collective-permute-done | bytes 1048608 | tf_op jit(solution)/shard_map/ppermute | solution.py:194
  249.0 3.6 add_add_fusion
  255.4 5.1 all-to-all-start.2
  261.0 4.0 fusion.6
  266.1 9.9 %concatenate.51.q_ref = bf16[4096,128]{1,0:T(8,128)(2,1)} concatenate(bf16[4096,64]{1,0:T(8,128)(2,1)} %bitcast.182, bf16[4096,4]{1,0:T(8,128)(2,1)} %get-tuple-element.150, bf16[4096,4]{1,0:T(8,128)(2,1)} %get-tuple-element.149, bf16[4096,4]{1,0:T(8,128)(2,1)} %get-tuple-element.148, bf16[4096,8]{1,0:T(8,128)(2,1)} %fusion.18, bf16[4096,1]{1,0:T(8,128)(2,1)} %get-tuple-element.129, ...), dimensions={1} | concatenate | bytes 2097152 | tf_op jit(solution)/shard_map/concatenate | solution.py:330
  276.0 2.4 copy.146
  278.3 2.5 multiply_reduce_fusion
  280.9 2.0 copy.147
  284.2 2.0 copy.148
  286.2 3.9 fusion.7
  291.2 6.7 concatenate.52.g_ref
  297.9 86.6 %shard_map.222 = (f32[8192,128]{1,0:T(8,128)}, f32[8192,128]{1,0:T(8,128)}, f32[4096,128]{1,0:T(8,128)}) custom-call(s32[16]{0:T(128)} %get-tuple-element.165.lo_ref, s32[16]{0:T(128)} %get-tuple-element.164.hi_ref, bf16[8192,128]{1,0:T(8,128)(2,1)} %concatenate.49.k_ref, bf16[8192,128]{1,0:T(8,128)(2,1)} %maximum_maximum_fusion.v_ref, ...), custom_call_target="tpu_custom_call" | custom-call | tf_op jit(solution)/shard_map/pallas_call | solution.py:139
  384.5 3.7 slice.263
  388.2 2.7 copy.151
  390.9 3.7 slice.264
  394.6 2.7 copy.150
  397.3 3.0 pad_maximum_fusion.1
  400.4 2.7 slice.265
  403.0 2.3 copy.152
  405.4 5.9 reduce-scatter.2.cloned.1.call-done
  411.3 2.6 pad_maximum_fusion.4
  413.9 6.1 all-to-all-start.3
  420.1 5.1 convolution_convert_fusion
  425.2 5.5 convert_bitcast_fusion
  430.8 1.8 convolution_convert_fusion.1
  432.5 22.4 %all-to-all-done.3 = bf16[8,512,192]{1,2,0:T(8,128)(2,1)} async-done(((bf16[8,512,192]{1,2,0:T(8,128)(2,1)}), bf16[8,512,192]{1,2,0:T(8,128)(2,1)}, u32[]{:S(2)}, u32[]{:S(2)}) %all-to-all-start.3) | async-done | bytes 1572896 | tf_op jit(solution)/shard_map/all_to_all | solution.py:285
  456.0 2.0 bitcast_convert_fusion
  463.7 3.6 convert_bitcast_fusion.1
  467.3 4.2 fusion.54
  473.2 2.5 select_reduce_fusion.1
  475.7 2.3 fusion.12
  482.7 3.9 collective-permute-done.1
  487.6 25.9 %psum.71 = f32[2,8]{1,0:T(2,128)} all-reduce(f32[2,8]{1,0:T(2,128)S(1)} %broadcast_multiply_fusion.4), channel_id=1, replica_groups=mesh['dp'=16,'tensor'=2] {'dp'}, use_global_device_ids=true, to_apply=%region_30.31 | all-reduce | flops 16 | bytes 128 | tf_op jit(solution)/shard_map/psum | solution.py:391
  513.7 48.4 %all-reduce = (f32[1024]{0:T(1024)}, f32[1024]{0:T(1024)}, f32[64]{0:T(128)}, f32[64]{0:T(128)}) all-reduce(f32[1024]{0:T(1024)S(1)} %get-tuple-element.96, f32[1024]{0:T(1024)S(1)} %get-tuple-element.94, f32[64]{0:T(128)S(1)} %reduce_sum.202, f32[64]{0:T(128)S(1)} %reduce_sum.205), channel_id=1, replica_groups=mesh['dp'=16,'tensor'=2] {'dp','tensor'}, use_global_device_ids=true, to_apply=%region_19.20 | all-reduce | flops 2176 | bytes 17408 | tf_op jit(solution)/shard_map/psum | solution.py:388
  562.1 2.9 add_add_fusion.1
  565.0 144.5 %all-reduce.4.cloned.1.call-done = (bf16[3,1024,512]{1,2,0:T(8,128)(2,1)}, bf16[2,1024,1408]{1,2,0:T(8,128)(2,1)}, bf16[512,1024]{1,0:T(8,128)(2,1)}, bf16[1408,1024]{1,0:T(8,128)(2,1)}) async-done(((bf16[3,1024,512]{1,2,0:T(8,128)(2,1)}, bf16[2,1024,1408]{1,2,0:T(8,128)(2,1)}, bf16[512,1024]{1,0:T(8,128)(2,1)}, bf16[1408,1024]{1,0:T(8,128)(2,1)}), (bf16[3,1024,512]{1,2,0:T(8,128)(2,1)}, ...) | async-done | bytes 12845072 | tf_op jit(solution)/shard_map/psum | solution.py:393
  709.5 5.4 copy.155
  714.9 2.8 convert_element_type.230
  717.7 9.1 %copy.156 = f32[2,1024,1408]{2,1,0:T(8,128)} copy(bf16[2,1024,1408]{1,2,0:T(8,128)(2,1)} %get-tuple-element.111) | data formatting | bytes 17301504
  726.8 5.1 convert_element_type.235
  (182 shorter events, 40.0 us)
Async XLA Ops:
  7.2 2.2 copy-start
  12.5 1.7 copy-start.15
  12.6 1.7 copy-start.36
  12.8 2.1 copy-start.9
  12.8 2.7 copy-start.7
  12.8 1.7 copy-start.33
  14.5 0.9 copy-start.31
  16.0 7.5 %copy-start.37 = (f32[2,8]{1,0:T(2,128)S(1)}, f32[2,8]{1,0:T(2,128)}, u32[]{:S(2)}) copy-start(f32[2,8]{1,0:T(2,128)} %param.27) | copy-start | bytes 196
  16.0 13.0 %copy-start.34 = (s32[512]{0:T(512)S(1)}, s32[512]{0:T(512)}, u32[]{:S(2)}) copy-start(s32[512]{0:T(512)} %param.17) | copy-start | bytes 6148
  16.0 13.0 %copy-start.35 = (s32[512]{0:T(512)S(1)}, s32[512]{0:T(512)}, u32[]{:S(2)}) copy-start(s32[512]{0:T(512)} %param.16) | copy-start | bytes 6148
  16.1 1.1 copy-start.22
  17.2 62.5 %all-to-all-start = ((bf16[8,512,192]{1,2,0:T(8,128)(2,1)}), bf16[8,512,192]{1,2,0:T(8,128)(2,1)}, u32[]{:S(2)}, u32[]{:S(2)}) async-start(bf16[8,512,192]{1,2,0:T(8,128)(2,1)} %bitcast.193), calls=%async_computation | async-start | bytes 3145728 | tf_op jit(solution)/shard_map/all_to_all | solution.py:190
  23.5 79.9 %all-gather.5.cloned.1.call-start = ((), (), s32[]{:S(2)}) async-start(), calls=%async_computation.6 | async-start | bytes 3145728 | tf_op jit(solution)/shard_map/all_gather | solution.py:223
  108.0 2.6 copy-start.6
  193.8 2.2 copy-start.18
  193.8 20.9 %copy-start.11 = (bf16[512,1024]{1,0:T(8,128)(2,1)S(1)}, bf16[512,1024]{1,0:T(8,128)(2,1)}, u32[]{:S(2)}) copy-start(bf16[512,1024]{1,0:T(8,128)(2,1)} %param.14) | copy-start | bytes 3145732
  196.0 18.7 %collective-permute-start = (bf16[512,1024]{1,0:T(8,128)(2,1)S(1)}, bf16[512,1024]{1,0:T(8,128)(2,1)S(1)}, u32[]{:S(2)}, u32[]{:S(2)}) collective-permute-start(bf16[512,1024]{1,0:T(8,128)(2,1)S(1)} %get-tuple-element.156), channel_id=1, source_target_pairs={{0,1},{1,0},{2,3},{3,2},{4,5},{5,4},{6,7},{7,6},{8,9},{9,8},{10,11... | collective-permute-start | bytes 3145736 | tf_op jit(solution)/shard_map/ppermute | solution.py:194
  214.7 0.7 copy-start.30
  215.2 14.2 %copy-start.1 = (f32[512,1024]{1,0:T(8,128)}, f32[512,1024]{1,0:T(8,128)S(1)}, u32[]{:S(2)}) copy-start(f32[512,1024]{1,0:T(8,128)S(1)} %get-tuple-element.115) | copy-start | bytes 6291460
  215.4 6.5 copy-start.23
  215.4 6.5 copy-start.38
  215.4 10.5 %slice-start = ((s8[5767168]{0:T(1024)(128)(4,1)}), s8[4194304]{0:T(1024)(128)(4,1)S(1)}, s32[]{:S(2)}) async-start(s8[5767168]{0:T(1024)(128)(4,1)} %bitcast.211), calls=%async_computation.8 | async-start | bytes 8388608
  221.9 4.0 slice-start.1
  225.8 3.5 copy-start.39
  225.8 3.5 copy-start.41
  229.3 1.7 copy-start.14
  231.0 18.0 %collective-permute-start.2 = (bf16[512,1024]{1,0:T(8,128)(2,1)}, bf16[512,1024]{1,0:T(8,128)(2,1)}, u32[]{:S(2)}, u32[]{:S(2)}) collective-permute-start(bf16[512,1024]{1,0:T(8,128)(2,1)} %fusion.46), channel_id=1, source_target_pairs={{0,1},{1,0},{2,3},{3,2},{4,5},{5,4},{6,7},{7,6},{8,9},{9,8},{10,11... | collective-permute-start | bytes 3145736 | tf_op jit(solution)/shard_map/ppermute | solution.py:194
  233.6 20.3 %copy-start.21 = (bf16[512,1024]{1,0:T(8,128)(2,1)S(1)}, bf16[512,1024]{1,0:T(8,128)(2,1)}, u32[]{:S(2)}) copy-start(bf16[512,1024]{1,0:T(8,128)(2,1)} %param.20) | copy-start | bytes 3145732
  252.5 1.3 copy-start.4
  255.4 20.6 %all-to-all-start.2 = ((bf16[8,512,64]{1,2,0:T(8,128)(2,1)}), bf16[8,512,64]{1,2,0:T(8,128)(2,1)}, u32[]{:S(2)}, u32[]{:S(2)}) async-start(bf16[8,512,64]{1,2,0:T(8,128)(2,1)} %bitcast.194), calls=%async_computation.2 | async-start | bytes 1048576 | tf_op jit(solution)/shard_map/all_to_all | solution.py:190
  260.5 150.7 %reduce-scatter.2.cloned.1.call-start = ((), (), s32[]{:S(2)}) async-start(), calls=%async_computation.5 | async-start | bytes 3145728 | tf_op jit(solution)/shard_map/reduce_scatter | solution.py:347
  413.9 41.1 %all-to-all-start.3 = ((bf16[8,512,192]{1,2,0:T(8,128)(2,1)}), bf16[8,512,192]{1,2,0:T(8,128)(2,1)}, u32[]{:S(2)}, u32[]{:S(2)}) async-start(bf16[8,512,192]{1,2,0:T(8,128)(2,1)} %pad_maximum_fusion.4), calls=%async_computation.4 | async-start | bytes 3145728 | tf_op jit(solution)/shard_map/all_to_all | solution.py:285
  419.9 289.6 %all-reduce.4.cloned.1.call-start = ((), (), s32[]{:S(2)}) async-start(), calls=%async_computation.7 | async-start | bytes 25690112 | tf_op jit(solution)/shard_map/psum | solution.py:393
  420.1 5.1 copy-start.2
  420.1 5.1 copy-start.40
  420.1 5.1 copy-start.42
  425.2 5.6 copy-start.5
  425.2 5.6 copy-start.19
  456.0 6.7 copy-start.24
  458.3 1.2 copy-start.10
  458.6 1.4 copy-start.8
  460.0 1.9 copy-start.16
  461.9 1.8 copy-start.12
  461.9 1.8 copy-start.32
  462.7 0.8 copy-start.26
  462.7 1.0 copy-start.28
  467.3 5.9 copy-start.20
  471.5 4.1 copy-start.13
  471.6 4.1 copy-start.25
  471.6 4.1 copy-start.27
  471.6 4.1 copy-start.29
  471.7 14.8 %collective-permute-start.1 = (bf16[512,512]{1,0:T(8,128)(2,1)S(1)}, bf16[512,512]{1,0:T(8,128)(2,1)S(1)}, u32[]{:S(2)}, u32[]{:S(2)}) collective-permute-start(bf16[512,512]{1,0:T(8,128)(2,1)S(1)} %dynamic-slice_convert_fusion.1), channel_id=1, source_target_pairs={{0,1},{1,0},{2,3},{3,2},{4,5},{5,4},{6,7},{7,6},{8,9},{9,8},{10,11... | collective-permute-start | bytes 1572872 | tf_op jit(solution)/shard_map/ppermute | solution.py:201
  478.0 8.5 %copy-start.3 = (f32[512,1024]{1,0:T(8,128)S(1)}, f32[512,1024]{1,0:T(8,128)}, u32[]{:S(2)}) copy-start(f32[512,1024]{1,0:T(8,128)} %copy-done.1) | copy-start | bytes 6291460
  478.5 1.3 copy-start.17
  480.7 81.4 %collective-permute-start.3 = (bf16[512,512]{1,0:T(8,128)(2,1)}, bf16[512,512]{1,0:T(8,128)(2,1)}, u32[]{:S(2)}, u32[]{:S(2)}) collective-permute-start(bf16[512,512]{1,0:T(8,128)(2,1)} %dynamic-slice_convert_fusion), channel_id=1, source_target_pairs={{0,1},{1,0},{2,3},{3,2},{4,5},{5,4},{6,7},{7,6},{8,9},{9,8},{10,11... | collective-permute-start | bytes 1572872 | tf_op jit(solution)/shard_map/ppermute | solution.py:201
Sparse Core Ops, SparseCore 0:
  84.4 9.9 all-gather.4
  400.5 10.7 reduce-scatter.1
  467.4 242.0 all-reduce.3
